TPU v7x, 256 devices: a whole 4x4x8 slice. The times are simulated.
256 devices in a mesh: section: 8 (over x, core), dom: 32 (over y, z).
Axes of the slice: x: 4, y: 4, z: 8, core: 2. Of those that a mesh axis runs over, the one named last changes fastest.
Arguments:
- node_latents: bfloat16 [8, 32768, 512], P('section', 'dom'), may hold values from -6 to 6
- edge_latents: bfloat16 [8, 49152, 512], P('section', 'dom'), may hold values from -6 to 6
- entering_nodes: bfloat16 [32768, 512], P('dom'), may hold values from -6 to 6
- entering_edges: bfloat16 [49152, 512], P('dom'), may hold values from -6 to 6
- edge_first: bfloat16 [8, 1536, 512], P('section'), may hold values from -0.15625 to 0.15625
- edge_second: bfloat16 [8, 512, 512], P('section'), may hold values from -0.25 to 0.25
- edge_gain: float32 [8, 512], P('section'), may hold values from 0.1 to 1.9
- node_first: bfloat16 [8, 1024, 512], P('section'), may hold values from -0.1875 to 0.1875
- node_second: bfloat16 [8, 512, 512], P('section'), may hold values from -0.25 to 0.25
- node_gain: float32 [8, 512], P('section'), may hold values from 0.1 to 1.9
- pair_list: int32 [32, 12, 3], P('dom'), may hold values from 0 to 7, as said below
- send_list: int32 [32, 4], P('dom'), may hold values from 0 to 7, as said below
- senders: int32 [49152, 128], P('dom'), may hold values from 0 to 1, as said below
- receivers: int32 [49152, 128], P('dom'), may hold values from 0 to 1, as said below
Outputs:
- final_nodes: bfloat16 [8, 32768, 512], P('section', 'dom')
- final_edges: bfloat16 [8, 49152, 512], P('section', 'dom')
Inputs may be any that keep to these rules, and one draw needn't show every extreme that they name: `pair_list`: columns 0 and 2 are node block numbers below 8, column 1 a partner code 0 to 4 (0: sender block on the same partition); every partition lists each code 1 to 4 at least once and names each of its node blocks in column 0 at least once. `send_list`: node block numbers below 8. `senders`: each row has exactly one 1. `receivers`: each row has exactly one 1.
All inputs are finite; a program needn't handle non-finite values.
Results may differ from a plain program's by a relative error of at most 0.0075.
Values may be sent and summed in bfloat16 or wider, within the bound.
A program may use at most 128 MiB of HBM per device.

v0:
```python
import functools

import jax
import jax.numpy as jnp
from jax import lax
from jax.experimental import pallas as pl
from jax.experimental.pallas import tpu as pltpu
from jax.sharding import PartitionSpec as P

OFFSETS = (1, -1, 2, -2)
EPSILON = 1e-05
MESH = pl.DeviceIdType.MESH
BF16 = jnp.bfloat16
F32 = jnp.float32
B = 128
ROWS = 256


def product(left, right):
    return jnp.dot(left, right, preferred_element_type=F32)


def layer_norm(values, gain):
    centred = values - jnp.mean(values, axis=-1, keepdims=True)
    spread = jnp.mean(centred * centred, axis=-1, keepdims=True)
    return centred * lax.rsqrt(spread + EPSILON) * gain


def blocks_of(step):
    return pl.ds(step * (ROWS // B), ROWS // B)


def flat(blocks):
    return blocks.reshape(blocks.shape[0] * blocks.shape[1], blocks.shape[2])


def split(rows):
    return rows.reshape(rows.shape[0] // B, B, rows.shape[1])


def rows_of(step, size=ROWS):
    return pl.ds(pl.multiple_of(step * size, size), size)


def kernel(
    n_sec, n_dom,
    nl, el, en, ee, wef_h, wes_h, ge, wnf_h, wns_h, gn, pairs, sends, snd_h, rcv_h,
    fn, fe,
    x0, e0, x1, e1, xo, eo, xf, ef, wef, wes, wnf, wns, snd, rcv,
    gsr, scat, look, pr, ew, xn, msg, own,
    stage0, stage1, inc0, inc1, part0, part1, ret0, ret1,
    load_sem, ent_sem, out_sem_x, out_sem_e,
    a_send, a_recv, c_send, c_recv, x_send, x_recv, e_send, e_recv,
):
    D = x0.shape[2]
    nb = x0.shape[0]
    kb = e0.shape[0] // B
    x_steps = x0.shape[0] * B // ROWS
    e_steps = e0.shape[0] // ROWS
    sec = lax.axis_index("section")
    dom = lax.axis_index("dom")
    nxt = lax.rem(sec + 1, n_sec)
    prv = lax.rem(sec + n_sec - 1, n_sec)

    loads = {}
    for i, (name, src, dst) in enumerate((
        ("x", nl, x0), ("wef", wef_h.at[0], wef), ("snd", snd_h, snd), ("rcv", rcv_h, rcv),
        ("e", el.at[0], e0), ("wes", wes_h.at[0], wes), ("wnf", wnf_h.at[0], wnf), ("wns", wns_h.at[0], wns),
    )):
        loads[name] = pltpu.make_async_copy(src, dst, load_sem.at[i])
        loads[name].start()
    enter_x = pltpu.make_async_copy(en, x1, ent_sem.at[0])
    enter_e = pltpu.make_async_copy(ee, e1, ent_sem.at[1])

    @pl.when(sec == 0)
    def _():
        enter_x.start()
        enter_e.start()

    barrier = pltpu.get_barrier_semaphore()
    for o in OFFSETS:
        pl.semaphore_signal(barrier, inc=1, device_id=(sec, lax.rem(dom + o + n_dom, n_dom)), device_id_type=MESH)
    pl.semaphore_signal(barrier, inc=1, device_id=(nxt, dom), device_id_type=MESH)
    pl.semaphore_signal(barrier, inc=1, device_id=(prv, dom), device_id_type=MESH)

    def forth(t, c):
        stage, inc = ((stage0, inc0), (stage1, inc1))[t]
        return pltpu.make_async_remote_copy(
            stage.at[c], inc.at[c], a_send.at[t, c], a_recv.at[t, c],
            device_id=(sec, lax.rem(dom + OFFSETS[c] + n_dom, n_dom)), device_id_type=MESH)

    def back(t, c):
        part, ret = ((part0, ret0), (part1, ret1))[t]
        return pltpu.make_async_remote_copy(
            part.at[c], ret.at[c], c_send.at[t, c], c_recv.at[t, c],
            device_id=(sec, lax.rem(dom - OFFSETS[c] + n_dom, n_dom)), device_id_type=MESH)

    def next_x(i):
        return pltpu.make_async_remote_copy(
            xo.at[blocks_of(i)], x1.at[blocks_of(i)], x_send.at[i], x_recv.at[i],
            device_id=(nxt, dom), device_id_type=MESH)

    def next_e(i):
        return pltpu.make_async_remote_copy(
            eo.at[rows_of(i)], e1.at[rows_of(i)], e_send.at[i], e_recv.at[i],
            device_id=(nxt, dom), device_id_type=MESH)

    def out_x(i):
        return pltpu.make_async_copy(xf.at[blocks_of(i)], fn.at[blocks_of(i)], out_sem_x.at[i])

    def out_e(i):
        return pltpu.make_async_copy(ef.at[rows_of(i)], fe.at[0, rows_of(i)], out_sem_e.at[i])

    def source(k):
        code = pairs[0, k, 1]
        return jnp.where(code == 0, pairs[0, k, 2], nb + code - 1)

    def send_blocks(t, x):
        for c in range(4):
            (stage0, stage1)[t][c] = x[sends[0, c]]
            forth(t, c).start()

    def tick(t, x, e, wait_e):
        last = t == 1
        inc = (inc0, inc1)[t]
        part = (part0, part1)[t]
        ret = (ret0, ret1)[t]
        x_new = (xo, xf)[t]
        e_new = (eo, ef)[t]

        def pre(i, _):
            r = blocks_of(i)
            xb = flat(x[r])
            look[r] = split(product(xb, wef[D : 2 * D, :]).astype(BF16))
            pr[r] = split(product(xb, wef[2 * D :, :]).astype(BF16))
            return 0

        lax.fori_loop(0, x_steps, pre, 0)
        wait_e()

        def edge_pre(i, _):
            r = rows_of(i)
            ew[r, :] = product(e[r, :], wef[0:D, :])
            return 0

        lax.fori_loop(0, e_steps, edge_pre, 0)
        if not last:
            loads["wnf"].wait()

        def node_pre(i, _):
            r = rows_of(i)
            xn[r, :] = product(flat(x[blocks_of(i)]), wnf[0:D, :])
            return 0

        lax.fori_loop(0, x_steps, node_pre, 0)
        if not last:
            loads["wes"].wait()
            loads["wns"].wait()
        for c in range(4):
            forth(t, c).wait_recv()
        for c in range(0, 4, 2):
            both = flat(inc[c : c + 2])
            look[nb + c : nb + c + 2] = split(product(both, wef[D : 2 * D, :]).astype(BF16))

        def edge(i, _):
            parts = []
            for j in range(ROWS // B):
                k = i * (ROWS // B) + j
                kr = rows_of(k, B)
                src = source(k)
                rcvb = pairs[0, k, 0]
                feats = jnp.concatenate([look[src], pr[rcvb]], axis=0)
                pre_act = ew[kr, :] + product(gsr[kr, :], feats)
                parts.append(jnp.maximum(pre_act, 0.0).astype(BF16))
            r = rows_of(i)
            message = layer_norm(product(jnp.concatenate(parts, axis=0), wes[...]), ge[...])
            msg[r, :] = message.astype(BF16)
            e_new[r, :] = (e[r, :].astype(F32) + message).astype(BF16)
            if last:
                out_e(i).start()
            else:
                @pl.when(sec < n_sec - 1)
                def _():
                    next_e(i).start()
            return 0

        lax.fori_loop(0, e_steps, edge, 0)
        for c in range(0, 4, 2):
            sums = product(scat[(nb + c) * B : (nb + c + 2) * B, :], msg[...]).astype(BF16)
            part[c] = sums[:B]
            part[c + 1] = sums[B:]
            back(t, c).start()
            back(t, c + 1).start()

        def own_sum(i, _):
            r = rows_of(i)
            own[r, :] = product(scat[r, :], msg[...])
            return 0

        lax.fori_loop(0, x_steps, own_sum, 0)
        for c in range(4):
            back(t, c).wait_recv()

        def node(i, _):
            r = rows_of(i)
            sums = []
            for j in range(ROWS // B):
                n = i * (ROWS // B) + j
                total = own[rows_of(n, B), :]
                for c in range(4):
                    total = total + jnp.where(sends[0, c] == n, 1.0, 0.0) * ret[c].astype(F32)
                sums.append(total.astype(BF16))
            agg = jnp.concatenate(sums, axis=0)
            hidden = jnp.maximum(xn[r, :] + product(agg, wnf[D:, :]), 0.0).astype(BF16)
            update = layer_norm(product(hidden, wns[...]), gn[...])
            x_new[blocks_of(i)] = split((flat(x[blocks_of(i)]).astype(F32) + update).astype(BF16))
            if last:
                out_x(i).start()
            else:
                @pl.when(sec < n_sec - 1)
                def _():
                    next_x(i).start()
            return 0

        lax.fori_loop(0, x_steps, node, 0)

    pl.semaphore_wait(barrier, 6)
    loads["x"].wait()
    send_blocks(0, x0)
    loads["snd"].wait()
    loads["rcv"].wait()

    def build(k, _):
        kr = rows_of(k, B)
        s_mat = snd[kr, :].astype(F32)
        r_mat = rcv[kr, :].astype(F32)
        gsr[kr, 0:B] = s_mat.astype(BF16)
        gsr[kr, B : 2 * B] = r_mat.astype(BF16)
        s_t = s_mat.T
        r_t = r_mat.T
        src = source(k)
        rcvb = pairs[0, k, 0]
        for n in range(nb + 4):
            block = s_t * jnp.where(src == n, 1.0, 0.0)
            if n < nb:
                block = block + r_t * jnp.where(rcvb == n, 1.0, 0.0)
            scat[n * B : (n + 1) * B, kr] = block.astype(BF16)
        return 0

    lax.fori_loop(0, kb, build, 0)
    loads["wef"].wait()
    tick(0, x0, e0, lambda: loads["e"].wait())

    @pl.when(sec == 0)
    def _():
        enter_x.wait()

    @pl.when(sec > 0)
    def _():
        for i in range(x_steps):
            next_x(i).wait_recv()

    send_blocks(1, x1)

    def wait_e1():
        @pl.when(sec == 0)
        def _():
            enter_e.wait()

        @pl.when(sec > 0)
        def _():
            for i in range(e_steps):
                next_e(i).wait_recv()

    tick(1, x1, e1, wait_e1)

    for i in range(x_steps):
        out_x(i).wait()
    for i in range(e_steps):
        out_e(i).wait()
    for t in range(2):
        for c in range(4):
            forth(t, c).wait_send()
            back(t, c).wait_send()

    @pl.when(sec < n_sec - 1)
    def _():
        for i in range(x_steps):
            next_x(i).wait_send()
        for i in range(e_steps):
            next_e(i).wait_send()


def local(n_sec, n_dom, *args):
    nl, el = args[0], args[1]
    n_rows, D = nl.shape[1:]
    e_rows = el.shape[1]
    nb = n_rows // B
    any_space = pl.BlockSpec(memory_space=pl.ANY)
    vmem = pl.BlockSpec(memory_space=pltpu.VMEM)
    smem = pl.BlockSpec(memory_space=pltpu.SMEM)
    specs = [any_space] * 14
    specs[6] = specs[9] = vmem
    specs[10] = specs[11] = smem
    nodes = pltpu.VMEM((nb, B, D), BF16)
    edges = pltpu.VMEM((e_rows, D), BF16)
    slots = pltpu.VMEM((4, B, D), BF16)
    dma = pltpu.SemaphoreType.DMA
    x_steps, e_steps = n_rows // ROWS, e_rows // ROWS
    args = (nl.reshape(nb, B, D), args[1], args[2].reshape(nb, B, D)) + args[3:]
    final_nodes, final_edges = pl.pallas_call(
        functools.partial(kernel, n_sec, n_dom),
        out_shape=(jax.ShapeDtypeStruct((nb, B, D), BF16), jax.ShapeDtypeStruct(el.shape, BF16)),
        in_specs=specs,
        out_specs=(any_space, any_space),
        scratch_shapes=[
            nodes, edges, nodes, edges, nodes, edges, nodes, edges,
            pltpu.VMEM((3 * D, D), BF16), pltpu.VMEM((D, D), BF16),
            pltpu.VMEM((2 * D, D), BF16), pltpu.VMEM((D, D), BF16),
            pltpu.VMEM((e_rows, B), jnp.int32), pltpu.VMEM((e_rows, B), jnp.int32),
            pltpu.VMEM((e_rows, 2 * B), BF16),
            pltpu.VMEM(((nb + 4) * B, e_rows), BF16),
            pltpu.VMEM((nb + 4, B, D), BF16),
            nodes,
            pltpu.VMEM((e_rows, D), F32),
            pltpu.VMEM((n_rows, D), F32),
            edges,
            pltpu.VMEM((n_rows, D), F32),
            slots, slots, slots, slots, slots, slots, slots, slots,
            dma((8,)), dma((2,)), dma((x_steps,)), dma((e_steps,)),
            dma((2, 4)), dma((2, 4)), dma((2, 4)), dma((2, 4)),
            dma((x_steps,)), dma((x_steps,)), dma((e_steps,)), dma((e_steps,)),
        ],
        compiler_params=pltpu.CompilerParams(
            collective_id=0, has_side_effects=True, vmem_limit_bytes=56 << 20),
    )(*args)
    return final_nodes.reshape(nl.shape), final_edges


def solution(mesh):
    placed = (
        P("section", "dom", None),
        P("section", "dom", None),
        P("dom", None),
        P("dom", None),
        P("section", None, None),
        P("section", None, None),
        P("section", None),
        P("section", None, None),
        P("section", None, None),
        P("section", None),
        P("dom", None, None),
        P("dom", None),
        P("dom", None),
        P("dom", None),
    )
    return jax.shard_map(
        functools.partial(local, mesh.shape["section"], mesh.shape["dom"]),
        mesh=mesh,
        in_specs=placed,
        out_specs=(P("section", "dom", None), P("section", "dom", None)),
        check_vma=False,
    )
```

profile of v0, /device:TPU:36, one launch (start us, length us, event | category | flops | bytes accessed | tf_op | source)
XLA Modules:
  0.0 84.1 jit_solution(9289649853906997512)
XLA Ops:
  0.6 1.4 %copy.16.pairs = s32[1,12,3]{2,1,0:T(8,128)} copy(s32[1,12,3]{1,0,2:T(1,128)} %param.24) | data formatting | bytes 288 | tf_op args[10]
  2.0 78.6 %shard_map.149 = (bf16[8,128,512]{2,1,0:T(8,128)(2,1)}, bf16[1,1536,512]{2,1,0:T(8,128)(2,1)}) custom-call(bf16[8,128,512]{2,1,0:T(8,128)(2,1)} %bitcast.4, bf16[1,1536,512]{2,1,0:T(8,128)(2,1)} %el.1, bf16[8,128,512]{2,1,0:T(8,128)(2,1)} %bitcast.5, bf16[1536,512]{1,0:T(8,128)(2,1)} %ee.1, bf16[1,1536,512]{2,1,0:T(8,128)(2,1)} %wef_h.1, ...), custom_call_target="tpu_custom_call" | custom-call | tf_op jit(solution)/shard_map/pallas_call | solution.py:311
  80.6 0.0 copy-start
  80.6 2.4 %copy.19 = bf16[1,1024,512]{2,1,0:T(8,128)(2,1)} copy(bf16[1,1024,512]{2,1,0:T(8,128)(2,1)} %bitcast.3) | data formatting | bytes 2097152
  83.0 0.0 copy-done
  83.0 1.1 %copy.20 = bf16[1,1536,512]{2,1,0:T(8,128)(2,1)} copy(bf16[1,1536,512]{2,1,0:T(8,128)(2,1)S(1)} %copy-done) | data formatting | bytes 3145728
Async XLA Ops:
  80.6 2.4 %copy-start = (bf16[1,1536,512]{2,1,0:T(8,128)(2,1)S(1)}, bf16[1,1536,512]{2,1,0:T(8,128)(2,1)}, u32[]{:S(2)}) copy-start(bf16[1,1536,512]{2,1,0:T(8,128)(2,1)} %get-tuple-element.9) | copy-start | bytes 4718596
where the time goes:
time: 84.3 us; the launch traced here: 84.1 us
  Pallas kernels  78.6 us (93%)
  local copies, waits for them, and re-layouts  4.89 us (6%)
    pallas_call x1, Pallas kernels, local(): pl.pallas_call(functools.partial(kernel, n_sec, n_dom), out_shape=(jax.Sh...  78.6 us
    unnamed x5, local copies, waits for them, and re-layouts  4.89 us

commit v1 on v0

--- a/solution.py
+++ b/solution.py
@@ -49,7 +49,7 @@
     x0, e0, x1, e1, xo, eo, xf, ef, wef, wes, wnf, wns, snd, rcv,
     gsr, scat, look, pr, ew, xn, msg, own,
     stage0, stage1, inc0, inc1, part0, part1, ret0, ret1,
-    load_sem, ent_sem, out_sem_x, out_sem_e,
+    go_sem, load_sem, ent_sem, out_sem_x, out_sem_e,
     a_send, a_recv, c_send, c_recv, x_send, x_recv, e_send, e_recv,
 ):
     D = x0.shape[2]
@@ -61,6 +61,8 @@
     dom = lax.axis_index("dom")
     nxt = lax.rem(sec + 1, n_sec)
     prv = lax.rem(sec + n_sec - 1, n_sec)
+    ahead = lax.rem(sec, 2) == 1
+    early = 2 * e_steps // 3
 
     loads = {}
     for i, (name, src, dst) in enumerate((
@@ -112,15 +114,15 @@
         return pltpu.make_async_copy(ef.at[rows_of(i)], fe.at[0, rows_of(i)], out_sem_e.at[i])
 
     def source(k):
-        code = pairs[0, k, 1]
-        return jnp.where(code == 0, pairs[0, k, 2], nb + code - 1)
+        code = pairs[1, 0, k]
+        return jnp.where(code == 0, pairs[2, 0, k], nb + code - 1)
 
     def send_blocks(t, x):
         for c in range(4):
             (stage0, stage1)[t][c] = x[sends[0, c]]
             forth(t, c).start()
 
-    def tick(t, x, e, wait_e):
+    def tick(t, x, e, ready_x, ready_e):
         last = t == 1
         inc = (inc0, inc1)[t]
         part = (part0, part1)[t]
@@ -129,30 +131,37 @@
         e_new = (eo, ef)[t]
 
         def pre(i, _):
+            ready_x(i)
             r = blocks_of(i)
             xb = flat(x[r])
             look[r] = split(product(xb, wef[D : 2 * D, :]).astype(BF16))
             pr[r] = split(product(xb, wef[2 * D :, :]).astype(BF16))
             return 0
 
-        lax.fori_loop(0, x_steps, pre, 0)
-        wait_e()
+        lax.fori_loop(0, x_steps, pre, 0, unroll=True)
+        if t == 0:
+            loads["e"].wait()
+
+            @pl.when(ahead)
+            def _():
+                for c in range(4):
+                    forth(0, c).wait_send()
+                pl.semaphore_signal(go_sem, inc=1, device_id=(sec - 1, dom), device_id_type=MESH)
+
+            @pl.when(jnp.logical_not(ahead))
+            def _():
+                pl.semaphore_wait(go_sem, 1)
+                send_blocks(0, x0)
+        else:
+            send_blocks(1, x1)
 
         def edge_pre(i, _):
+            ready_e(i)
             r = rows_of(i)
             ew[r, :] = product(e[r, :], wef[0:D, :])
             return 0
 
-        lax.fori_loop(0, e_steps, edge_pre, 0)
-        if not last:
-            loads["wnf"].wait()
-
-        def node_pre(i, _):
-            r = rows_of(i)
-            xn[r, :] = product(flat(x[blocks_of(i)]), wnf[0:D, :])
-            return 0
-
-        lax.fori_loop(0, x_steps, node_pre, 0)
+        lax.fori_loop(0, e_steps, edge_pre, 0, unroll=True)
         if not last:
             loads["wes"].wait()
             loads["wns"].wait()
@@ -168,7 +177,7 @@
                 k = i * (ROWS // B) + j
                 kr = rows_of(k, B)
                 src = source(k)
-                rcvb = pairs[0, k, 0]
+                rcvb = pairs[0, 0, k]
                 feats = jnp.concatenate([look[src], pr[rcvb]], axis=0)
                 pre_act = ew[kr, :] + product(gsr[kr, :], feats)
                 parts.append(jnp.maximum(pre_act, 0.0).astype(BF16))
@@ -179,12 +188,12 @@
             if last:
                 out_e(i).start()
             else:
-                @pl.when(sec < n_sec - 1)
+                @pl.when(jnp.logical_and(sec < n_sec - 1, i < early))
                 def _():
                     next_e(i).start()
             return 0
 
-        lax.fori_loop(0, e_steps, edge, 0)
+        lax.fori_loop(0, e_steps, edge, 0, unroll=True)
         for c in range(0, 4, 2):
             sums = product(scat[(nb + c) * B : (nb + c + 2) * B, :], msg[...]).astype(BF16)
             part[c] = sums[:B]
@@ -197,7 +206,16 @@
             own[r, :] = product(scat[r, :], msg[...])
             return 0
 
-        lax.fori_loop(0, x_steps, own_sum, 0)
+        lax.fori_loop(0, x_steps, own_sum, 0, unroll=True)
+        if not last:
+            loads["wnf"].wait()
+
+        def node_pre(i, _):
+            r = rows_of(i)
+            xn[r, :] = product(flat(x[blocks_of(i)]), wnf[0:D, :])
+            return 0
+
+        lax.fori_loop(0, x_steps, node_pre, 0, unroll=True)
         for c in range(4):
             back(t, c).wait_recv()
 
@@ -222,11 +240,20 @@
                     next_x(i).start()
             return 0
 
-        lax.fori_loop(0, x_steps, node, 0)
+        lax.fori_loop(0, x_steps, node, 0, unroll=True)
+        if not last:
+            @pl.when(sec < n_sec - 1)
+            def _():
+                for i in range(early, e_steps):
+                    next_e(i).start()
 
     pl.semaphore_wait(barrier, 6)
     loads["x"].wait()
-    send_blocks(0, x0)
+
+    @pl.when(ahead)
+    def _():
+        send_blocks(0, x0)
+
     loads["snd"].wait()
     loads["rcv"].wait()
 
@@ -239,7 +266,7 @@
         s_t = s_mat.T
         r_t = r_mat.T
         src = source(k)
-        rcvb = pairs[0, k, 0]
+        rcvb = pairs[0, 0, k]
         for n in range(nb + 4):
             block = s_t * jnp.where(src == n, 1.0, 0.0)
             if n < nb:
@@ -249,39 +276,38 @@
 
     lax.fori_loop(0, kb, build, 0)
     loads["wef"].wait()
-    tick(0, x0, e0, lambda: loads["e"].wait())
+    tick(0, x0, e0, lambda i: None, lambda i: None)
 
     @pl.when(sec == 0)
     def _():
         enter_x.wait()
-
-    @pl.when(sec > 0)
-    def _():
-        for i in range(x_steps):
-            next_x(i).wait_recv()
-
-    send_blocks(1, x1)
-
-    def wait_e1():
-        @pl.when(sec == 0)
-        def _():
-            enter_e.wait()
-
+        enter_e.wait()
+
+    def ready_x(i):
         @pl.when(sec > 0)
         def _():
-            for i in range(e_steps):
-                next_e(i).wait_recv()
-
-    tick(1, x1, e1, wait_e1)
+            next_x(i).wait_recv()
+
+    def ready_e(i):
+        @pl.when(sec > 0)
+        def _():
+            next_e(i).wait_recv()
+
+    tick(1, x1, e1, ready_x, ready_e)
 
     for i in range(x_steps):
         out_x(i).wait()
     for i in range(e_steps):
         out_e(i).wait()
-    for t in range(2):
+    for c in range(4):
+        forth(1, c).wait_send()
+        back(0, c).wait_send()
+        back(1, c).wait_send()
+
+    @pl.when(jnp.logical_not(ahead))
+    def _():
         for c in range(4):
-            forth(t, c).wait_send()
-            back(t, c).wait_send()
+            forth(0, c).wait_send()
 
     @pl.when(sec < n_sec - 1)
     def _():
@@ -307,7 +333,8 @@
     slots = pltpu.VMEM((4, B, D), BF16)
     dma = pltpu.SemaphoreType.DMA
     x_steps, e_steps = n_rows // ROWS, e_rows // ROWS
-    args = (nl.reshape(nb, B, D), args[1], args[2].reshape(nb, B, D)) + args[3:]
+    pairs = jnp.transpose(args[10], (2, 0, 1))
+    args = (nl.reshape(nb, B, D), args[1], args[2].reshape(nb, B, D)) + args[3:10] + (pairs,) + args[11:]
     final_nodes, final_edges = pl.pallas_call(
         functools.partial(kernel, n_sec, n_dom),
         out_shape=(jax.ShapeDtypeStruct((nb, B, D), BF16), jax.ShapeDtypeStruct(el.shape, BF16)),
@@ -327,7 +354,7 @@
             edges,
             pltpu.VMEM((n_rows, D), F32),
             slots, slots, slots, slots, slots, slots, slots, slots,
-            dma((8,)), dma((2,)), dma((x_steps,)), dma((e_steps,)),
+            pltpu.SemaphoreType.REGULAR, dma((8,)), dma((2,)), dma((x_steps,)), dma((e_steps,)),
             dma((2, 4)), dma((2, 4)), dma((2, 4)), dma((2, 4)),
             dma((x_steps,)), dma((x_steps,)), dma((e_steps,)), dma((e_steps,)),
         ],

time: 84.3 us -> 75.9 us (0.900)
  the two profiles are of different devices: /device:TPU:36 before, /device:TPU:1 now
where the time goes in v1:
time: 75.9 us; the launch traced here: 75.7 us
  Pallas kernels  71.6 us (94%)
  local copies, waits for them, and re-layouts  3.53 us (5%)
    pallas_call x1, Pallas kernels, local(): pl.pallas_call(functools.partial(kernel, n_sec, n_dom), out_shape=(jax.Sh...  71.6 us
    unnamed x4, local copies, waits for them, and re-layouts  3.53 us

profile of v1, /device:TPU:1, one launch (start us, length us, event | category | flops | bytes accessed | tf_op | source)
XLA Modules:
  0.0 75.7 jit_solution(12198266072395536051)
XLA Ops:
  0.6 71.6 %shard_map.149 = (bf16[8,128,512]{2,1,0:T(8,128)(2,1)}, bf16[1,1536,512]{2,1,0:T(8,128)(2,1)}) custom-call(bf16[8,128,512]{2,1,0:T(8,128)(2,1)} %bitcast.5, bf16[1,1536,512]{2,1,0:T(8,128)(2,1)} %el.1, bf16[8,128,512]{2,1,0:T(8,128)(2,1)} %bitcast.6, bf16[1536,512]{1,0:T(8,128)(2,1)} %ee.1, bf16[1,1536,512]{2,1,0:T(8,128)(2,1)} %wef_h.1, ...), custom_call_target="tpu_custom_call" | custom-call | tf_op jit(solution)/shard_map/pallas_call | solution.py:338
  72.2 0.0 copy-start
  72.2 2.4 %copy.18 = bf16[1,1024,512]{2,1,0:T(8,128)(2,1)} copy(bf16[1,1024,512]{2,1,0:T(8,128)(2,1)} %bitcast.4) | data formatting | bytes 2097152
  74.6 0.0 copy-done
  74.6 1.1 %copy.19 = bf16[1,1536,512]{2,1,0:T(8,128)(2,1)} copy(bf16[1,1536,512]{2,1,0:T(8,128)(2,1)S(1)} %copy-done) | data formatting | bytes 3145728
Async XLA Ops:
  72.2 2.4 %copy-start = (bf16[1,1536,512]{2,1,0:T(8,128)(2,1)S(1)}, bf16[1,1536,512]{2,1,0:T(8,128)(2,1)}, u32[]{:S(2)}) copy-start(bf16[1,1536,512]{2,1,0:T(8,128)(2,1)} %get-tuple-element.9) | copy-start | bytes 4718596

commit v2 on v1

--- a/solution.py
+++ b/solution.py
@@ -62,22 +62,17 @@
     nxt = lax.rem(sec + 1, n_sec)
     prv = lax.rem(sec + n_sec - 1, n_sec)
     ahead = lax.rem(sec, 2) == 1
-    early = 2 * e_steps // 3
+    early = e_steps // 2
 
     loads = {}
     for i, (name, src, dst) in enumerate((
-        ("x", nl, x0), ("wef", wef_h.at[0], wef), ("snd", snd_h, snd), ("rcv", rcv_h, rcv),
+        ("x", nl, x0), ("snd", snd_h, snd), ("rcv", rcv_h, rcv), ("wef", wef_h.at[0], wef),
         ("e", el.at[0], e0), ("wes", wes_h.at[0], wes), ("wnf", wnf_h.at[0], wnf), ("wns", wns_h.at[0], wns),
     )):
         loads[name] = pltpu.make_async_copy(src, dst, load_sem.at[i])
-        loads[name].start()
     enter_x = pltpu.make_async_copy(en, x1, ent_sem.at[0])
     enter_e = pltpu.make_async_copy(ee, e1, ent_sem.at[1])
-
-    @pl.when(sec == 0)
-    def _():
-        enter_x.start()
-        enter_e.start()
+    loads["x"].start()
 
     barrier = pltpu.get_barrier_semaphore()
     for o in OFFSETS:
@@ -131,14 +126,19 @@
         e_new = (eo, ef)[t]
 
         def pre(i, _):
-            ready_x(i)
             r = blocks_of(i)
             xb = flat(x[r])
             look[r] = split(product(xb, wef[D : 2 * D, :]).astype(BF16))
             pr[r] = split(product(xb, wef[2 * D :, :]).astype(BF16))
             return 0
 
-        lax.fori_loop(0, x_steps, pre, 0, unroll=True)
+        for i in range(x_steps):
+            ready_x(i)
+            if last and i == x_steps - 1:
+                @pl.when(sec > 0)
+                def _():
+                    send_blocks(1, x1)
+            pre(i, 0)
         if t == 0:
             loads["e"].wait()
 
@@ -152,8 +152,6 @@
             def _():
                 pl.semaphore_wait(go_sem, 1)
                 send_blocks(0, x0)
-        else:
-            send_blocks(1, x1)
 
         def edge_pre(i, _):
             ready_e(i)
@@ -167,6 +165,11 @@
             loads["wns"].wait()
         for c in range(4):
             forth(t, c).wait_recv()
+        if not last:
+            @pl.when(sec == 0)
+            def _():
+                enter_x.wait()
+                send_blocks(1, x1)
         for c in range(0, 4, 2):
             both = flat(inc[c : c + 2])
             look[nb + c : nb + c + 2] = split(product(both, wef[D : 2 * D, :]).astype(BF16))
@@ -247,8 +250,16 @@
                 for i in range(early, e_steps):
                     next_e(i).start()
 
+    loads["x"].wait()
+    for name in ("snd", "rcv", "wef", "e", "wes", "wnf", "wns"):
+        loads[name].start()
+
+    @pl.when(sec == 0)
+    def _():
+        enter_x.start()
+        enter_e.start()
+
     pl.semaphore_wait(barrier, 6)
-    loads["x"].wait()
 
     @pl.when(ahead)
     def _():
@@ -274,13 +285,12 @@
             scat[n * B : (n + 1) * B, kr] = block.astype(BF16)
         return 0
 
-    lax.fori_loop(0, kb, build, 0)
+    lax.fori_loop(0, kb, build, 0, unroll=2)
     loads["wef"].wait()
     tick(0, x0, e0, lambda i: None, lambda i: None)
 
     @pl.when(sec == 0)
     def _():
-        enter_x.wait()
         enter_e.wait()
 
     def ready_x(i):
@@ -315,6 +325,36 @@
             next_x(i).wait_send()
         for i in range(e_steps):
             next_e(i).wait_send()
+
+
+def hand_over_kernel(nodes, edges, out_nodes, out_edges, buf, in_sem, out_sem):
+    size = 2 * ROWS
+    parts = [(src, dst, r) for src, dst in ((nodes, out_nodes), (edges, out_edges)) for r in range(0, src.shape[1], size)]
+    reads = [
+        pltpu.make_async_copy(src.at[0, pl.ds(r, size)], buf.at[i], in_sem.at[i]) for i, (src, _, r) in enumerate(parts)]
+    writes = [
+        pltpu.make_async_copy(buf.at[i], dst.at[0, pl.ds(r, size)], out_sem.at[i]) for i, (_, dst, r) in enumerate(parts)]
+    for copy in reads:
+        copy.start()
+    for read, write in zip(reads, writes):
+        read.wait()
+        write.start()
+    for copy in writes:
+        copy.wait()
+
+
+def hand_over(nodes, edges):
+    any_space = pl.BlockSpec(memory_space=pl.ANY)
+    count = (nodes.shape[1] + edges.shape[1]) // (2 * ROWS)
+    return pl.pallas_call(
+        hand_over_kernel,
+        out_shape=(jax.ShapeDtypeStruct(nodes.shape, BF16), jax.ShapeDtypeStruct(edges.shape, BF16)),
+        in_specs=[any_space] * 2,
+        out_specs=(any_space,) * 2,
+        scratch_shapes=[
+            pltpu.VMEM((count, 2 * ROWS, nodes.shape[2]), BF16),
+            pltpu.SemaphoreType.DMA((count,)), pltpu.SemaphoreType.DMA((count,))],
+    )(nodes, edges)
 
 
 def local(n_sec, n_dom, *args):
@@ -361,7 +401,7 @@
         compiler_params=pltpu.CompilerParams(
             collective_id=0, has_side_effects=True, vmem_limit_bytes=56 << 20),
     )(*args)
-    return final_nodes.reshape(nl.shape), final_edges
+    return hand_over(final_nodes.reshape(nl.shape), final_edges)
 
 
 def solution(mesh):

time: 75.9 us -> 72 us (0.949)
  the two profiles are of different devices: /device:TPU:1 before, /device:TPU:2 now
where the time goes in v2:
time: 72 us; the launch traced here: 71.8 us
  Pallas kernels  71 us (99%)
  between operations  0.8 us (1%)
    pallas_call x1, Pallas kernels, local(): pl.pallas_call(functools.partial(kernel, n_sec, n_dom), out_shape=(jax.Sh...  68.4 us
    pallas_call x1, Pallas kernels, hand_over(): pl.pallas_call(hand_over_kernel, out_shape=(jax.ShapeDtypeStruct(nodes.sh...  2.61 us

profile of v2, /device:TPU:2, one launch (start us, length us, event | category | flops | bytes accessed | tf_op | source)
XLA Modules:
  0.0 71.8 jit_solution(1757042814544544885)
XLA Ops:
  0.6 68.4 %shard_map.149 = (bf16[8,128,512]{2,1,0:T(8,128)(2,1)}, bf16[1,1536,512]{2,1,0:T(8,128)(2,1)}) custom-call(bf16[8,128,512]{2,1,0:T(8,128)(2,1)} %bitcast.5, bf16[1,1536,512]{2,1,0:T(8,128)(2,1)} %el.1, bf16[8,128,512]{2,1,0:T(8,128)(2,1)} %bitcast.6, bf16[1536,512]{1,0:T(8,128)(2,1)} %ee.1, bf16[1,1536,512]{2,1,0:T(8,128)(2,1)} %wef_h.1, ...), custom_call_target="tpu_custom_call" | custom-call | tf_op jit(solution)/shard_map/pallas_call | solution.py:378
  69.0 2.6 %shard_map.150 = (bf16[1,1024,512]{2,1,0:T(8,128)(2,1)}, bf16[1,1536,512]{2,1,0:T(8,128)(2,1)}) custom-call(bf16[1,1024,512]{2,1,0:T(8,128)(2,1)} %bitcast.4, bf16[1,1536,512]{2,1,0:T(8,128)(2,1)} %get-tuple-element.5.edges), custom_call_target="tpu_custom_call" | custom-call | tf_op jit(solution)/shard_map/pallas_call | solution.py:349

commit v3 on v2

--- a/solution.py
+++ b/solution.py
@@ -45,11 +45,11 @@
 def kernel(
     n_sec, n_dom,
     nl, el, en, ee, wef_h, wes_h, ge, wnf_h, wns_h, gn, pairs, sends, snd_h, rcv_h,
-    fn, fe,
-    x0, e0, x1, e1, xo, eo, xf, ef, wef, wes, wnf, wns, snd, rcv,
+    xf, ef,
+    x0, e0, x1, e1, xo, eo, wef, wes, wnf, wns, snd, rcv,
     gsr, scat, look, pr, ew, xn, msg, own,
     stage0, stage1, inc0, inc1, part0, part1, ret0, ret1,
-    go_sem, load_sem, ent_sem, out_sem_x, out_sem_e,
+    go_sem, load_sem, ent_sem,
     a_send, a_recv, c_send, c_recv, x_send, x_recv, e_send, e_recv,
 ):
     D = x0.shape[2]
@@ -101,12 +101,6 @@
         return pltpu.make_async_remote_copy(
             eo.at[rows_of(i)], e1.at[rows_of(i)], e_send.at[i], e_recv.at[i],
             device_id=(nxt, dom), device_id_type=MESH)
-
-    def out_x(i):
-        return pltpu.make_async_copy(xf.at[blocks_of(i)], fn.at[blocks_of(i)], out_sem_x.at[i])
-
-    def out_e(i):
-        return pltpu.make_async_copy(ef.at[rows_of(i)], fe.at[0, rows_of(i)], out_sem_e.at[i])
 
     def source(k):
         code = pairs[1, 0, k]
@@ -174,7 +168,7 @@
             both = flat(inc[c : c + 2])
             look[nb + c : nb + c + 2] = split(product(both, wef[D : 2 * D, :]).astype(BF16))
 
-        def edge(i, _):
+        def edge(i):
             parts = []
             for j in range(ROWS // B):
                 k = i * (ROWS // B) + j
@@ -188,15 +182,14 @@
             message = layer_norm(product(jnp.concatenate(parts, axis=0), wes[...]), ge[...])
             msg[r, :] = message.astype(BF16)
             e_new[r, :] = (e[r, :].astype(F32) + message).astype(BF16)
-            if last:
-                out_e(i).start()
-            else:
-                @pl.when(jnp.logical_and(sec < n_sec - 1, i < early))
+
+        for i in range(e_steps):
+            edge(i)
+            if not last and i == early - 1:
+                @pl.when(sec < n_sec - 1)
                 def _():
-                    next_e(i).start()
-            return 0
-
-        lax.fori_loop(0, e_steps, edge, 0, unroll=True)
+                    for j in range(early):
+                        next_e(j).start()
         for c in range(0, 4, 2):
             sums = product(scat[(nb + c) * B : (nb + c + 2) * B, :], msg[...]).astype(BF16)
             part[c] = sums[:B]
@@ -222,7 +215,7 @@
         for c in range(4):
             back(t, c).wait_recv()
 
-        def node(i, _):
+        def node(i):
             r = rows_of(i)
             sums = []
             for j in range(ROWS // B):
@@ -235,15 +228,14 @@
             hidden = jnp.maximum(xn[r, :] + product(agg, wnf[D:, :]), 0.0).astype(BF16)
             update = layer_norm(product(hidden, wns[...]), gn[...])
             x_new[blocks_of(i)] = split((flat(x[blocks_of(i)]).astype(F32) + update).astype(BF16))
-            if last:
-                out_x(i).start()
-            else:
+
+        for i in range(x_steps):
+            node(i)
+            if not last and i % 2 == 1:
                 @pl.when(sec < n_sec - 1)
                 def _():
+                    next_x(i - 1).start()
                     next_x(i).start()
-            return 0
-
-        lax.fori_loop(0, x_steps, node, 0, unroll=True)
         if not last:
             @pl.when(sec < n_sec - 1)
             def _():
@@ -305,10 +297,6 @@
 
     tick(1, x1, e1, ready_x, ready_e)
 
-    for i in range(x_steps):
-        out_x(i).wait()
-    for i in range(e_steps):
-        out_e(i).wait()
     for c in range(4):
         forth(1, c).wait_send()
         back(0, c).wait_send()
@@ -325,36 +313,6 @@
             next_x(i).wait_send()
         for i in range(e_steps):
             next_e(i).wait_send()
-
-
-def hand_over_kernel(nodes, edges, out_nodes, out_edges, buf, in_sem, out_sem):
-    size = 2 * ROWS
-    parts = [(src, dst, r) for src, dst in ((nodes, out_nodes), (edges, out_edges)) for r in range(0, src.shape[1], size)]
-    reads = [
-        pltpu.make_async_copy(src.at[0, pl.ds(r, size)], buf.at[i], in_sem.at[i]) for i, (src, _, r) in enumerate(parts)]
-    writes = [
-        pltpu.make_async_copy(buf.at[i], dst.at[0, pl.ds(r, size)], out_sem.at[i]) for i, (_, dst, r) in enumerate(parts)]
-    for copy in reads:
-        copy.start()
-    for read, write in zip(reads, writes):
-        read.wait()
-        write.start()
-    for copy in writes:
-        copy.wait()
-
-
-def hand_over(nodes, edges):
-    any_space = pl.BlockSpec(memory_space=pl.ANY)
-    count = (nodes.shape[1] + edges.shape[1]) // (2 * ROWS)
-    return pl.pallas_call(
-        hand_over_kernel,
-        out_shape=(jax.ShapeDtypeStruct(nodes.shape, BF16), jax.ShapeDtypeStruct(edges.shape, BF16)),
-        in_specs=[any_space] * 2,
-        out_specs=(any_space,) * 2,
-        scratch_shapes=[
-            pltpu.VMEM((count, 2 * ROWS, nodes.shape[2]), BF16),
-            pltpu.SemaphoreType.DMA((count,)), pltpu.SemaphoreType.DMA((count,))],
-    )(nodes, edges)
 
 
 def local(n_sec, n_dom, *args):
@@ -377,11 +335,11 @@
     args = (nl.reshape(nb, B, D), args[1], args[2].reshape(nb, B, D)) + args[3:10] + (pairs,) + args[11:]
     final_nodes, final_edges = pl.pallas_call(
         functools.partial(kernel, n_sec, n_dom),
-        out_shape=(jax.ShapeDtypeStruct((nb, B, D), BF16), jax.ShapeDtypeStruct(el.shape, BF16)),
+        out_shape=(pltpu.VMEM((nb, B, D), BF16), pltpu.VMEM((e_rows, D), BF16)),
         in_specs=specs,
-        out_specs=(any_space, any_space),
+        out_specs=(vmem, vmem),
         scratch_shapes=[
-            nodes, edges, nodes, edges, nodes, edges, nodes, edges,
+            nodes, edges, nodes, edges, nodes, edges,
             pltpu.VMEM((3 * D, D), BF16), pltpu.VMEM((D, D), BF16),
             pltpu.VMEM((2 * D, D), BF16), pltpu.VMEM((D, D), BF16),
             pltpu.VMEM((e_rows, B), jnp.int32), pltpu.VMEM((e_rows, B), jnp.int32),
@@ -394,14 +352,14 @@
             edges,
             pltpu.VMEM((n_rows, D), F32),
             slots, slots, slots, slots, slots, slots, slots, slots,
-            pltpu.SemaphoreType.REGULAR, dma((8,)), dma((2,)), dma((x_steps,)), dma((e_steps,)),
+            pltpu.SemaphoreType.REGULAR, dma((8,)), dma((2,)),
             dma((2, 4)), dma((2, 4)), dma((2, 4)), dma((2, 4)),
             dma((x_steps,)), dma((x_steps,)), dma((e_steps,)), dma((e_steps,)),
         ],
         compiler_params=pltpu.CompilerParams(
             collective_id=0, has_side_effects=True, vmem_limit_bytes=56 << 20),
     )(*args)
-    return hand_over(final_nodes.reshape(nl.shape), final_edges)
+    return final_nodes.reshape(nl.shape), final_edges.reshape(el.shape)
 
 
 def solution(mesh):

time: 72 us -> 69.9 us (0.971)
  Pallas kernels: 71 us -> 67 us
  local copies, waits for them, and re-layouts: 0 us -> 2.11 us
    pallas_call x2 -> x1, Pallas kernels: 71 us -> 67 us  [local(): pl.pallas_call(functools.partial(kernel, n_sec, n_dom), out_shape=(pltpu....]
    unnamed x0 -> x2, local copies, waits for them, and re-layouts: none -> 2.11 us
where the time goes in v3:
time: 69.9 us; the launch traced here: 69.8 us
  Pallas kernels  67 us (96%)
  local copies, waits for them, and re-layouts  2.11 us (3%)
    pallas_call x1, Pallas kernels, local(): pl.pallas_call(functools.partial(kernel, n_sec, n_dom), out_shape=(pltpu....  67 us
    unnamed x2, local copies, waits for them, and re-layouts  2.11 us

profile of v3, /device:TPU:2, one launch (start us, length us, event | category | flops | bytes accessed | tf_op | source)
XLA Modules:
  0.0 69.8 jit_solution(2781993918923628174)
XLA Ops:
  0.6 67.0 %shard_map.149 = (bf16[8,128,512]{2,1,0:T(8,128)(2,1)S(1)}, bf16[1536,512]{1,0:T(8,128)(2,1)S(1)}) custom-call(bf16[8,128,512]{2,1,0:T(8,128)(2,1)} %bitcast.7, bf16[1,1536,512]{2,1,0:T(8,128)(2,1)} %el.1, bf16[8,128,512]{2,1,0:T(8,128)(2,1)} %bitcast.8, bf16[1536,512]{1,0:T(8,128)(2,1)} %ee.1, bf16[1,1536,512]{2,1,0:T(8,128)(2,1)} %wef_h.1, ...), custom_call_target="tpu_custom_call" | custom-call | tf_op jit(solution)/shard_map/pallas_call | solution.py:336
  67.6 1.0 %copy.18 = bf16[1,1024,512]{2,1,0:T(8,128)(2,1)} copy(bf16[1,1024,512]{2,1,0:T(8,128)(2,1)S(1)} %bitcast.6) | data formatting | bytes 2097152
  68.6 1.1 %copy.19 = bf16[1,1536,512]{2,1,0:T(8,128)(2,1)} copy(bf16[1,1536,512]{2,1,0:T(8,128)(2,1)S(1)} %bitcast.5) | data formatting | bytes 3145728

commit v4 on v3

--- a/solution.py
+++ b/solution.py
@@ -147,6 +147,14 @@
                 pl.semaphore_wait(go_sem, 1)
                 send_blocks(0, x0)
 
+        if last:
+            @pl.when(sec < n_sec - 1)
+            def _():
+                for i in range(x_steps):
+                    next_x(i).wait_send()
+                for i in range(early, e_steps):
+                    next_e(i).start()
+
         def edge_pre(i, _):
             ready_e(i)
             r = rows_of(i)
@@ -159,11 +167,6 @@
             loads["wns"].wait()
         for c in range(4):
             forth(t, c).wait_recv()
-        if not last:
-            @pl.when(sec == 0)
-            def _():
-                enter_x.wait()
-                send_blocks(1, x1)
         for c in range(0, 4, 2):
             both = flat(inc[c : c + 2])
             look[nb + c : nb + c + 2] = split(product(both, wef[D : 2 * D, :]).astype(BF16))
@@ -214,6 +217,11 @@
         lax.fori_loop(0, x_steps, node_pre, 0, unroll=True)
         for c in range(4):
             back(t, c).wait_recv()
+        if not last:
+            @pl.when(sec == 0)
+            def _():
+                enter_x.wait()
+                send_blocks(1, x1)
 
         def node(i):
             r = rows_of(i)
@@ -231,16 +239,11 @@
 
         for i in range(x_steps):
             node(i)
-            if not last and i % 2 == 1:
+            if not last and i in (0, x_steps - 1):
                 @pl.when(sec < n_sec - 1)
                 def _():
-                    next_x(i - 1).start()
-                    next_x(i).start()
-        if not last:
-            @pl.when(sec < n_sec - 1)
-            def _():
-                for i in range(early, e_steps):
-                    next_e(i).start()
+                    for j in range(min(i, 1), i + 1):
+                        next_x(j).start()
 
     loads["x"].wait()
     for name in ("snd", "rcv", "wef", "e", "wes", "wnf", "wns"):
@@ -309,8 +312,6 @@
 
     @pl.when(sec < n_sec - 1)
     def _():
-        for i in range(x_steps):
-            next_x(i).wait_send()
         for i in range(e_steps):
             next_e(i).wait_send()
 

time: 69.9 us -> 69.6 us (level)
  no operation moved by 1% of the time
where the time goes in v4:
time: 69.6 us; the launch traced here: 69.5 us
  Pallas kernels  66.7 us (96%)
  local copies, waits for them, and re-layouts  2.11 us (3%)
    pallas_call x1, Pallas kernels, local(): pl.pallas_call(functools.partial(kernel, n_sec, n_dom), out_shape=(pltpu....  66.7 us
    unnamed x2, local copies, waits for them, and re-layouts  2.11 us

profile of v4, /device:TPU:2, one launch (start us, length us, event | category | flops | bytes accessed | tf_op | source)
XLA Modules:
  0.0 69.5 jit_solution(6828222451107929954)
XLA Ops:
  0.6 66.7 %shard_map.149 = (bf16[8,128,512]{2,1,0:T(8,128)(2,1)S(1)}, bf16[1536,512]{1,0:T(8,128)(2,1)S(1)}) custom-call(bf16[8,128,512]{2,1,0:T(8,128)(2,1)} %bitcast.7, bf16[1,1536,512]{2,1,0:T(8,128)(2,1)} %el.1, bf16[8,128,512]{2,1,0:T(8,128)(2,1)} %bitcast.8, bf16[1536,512]{1,0:T(8,128)(2,1)} %ee.1, bf16[1,1536,512]{2,1,0:T(8,128)(2,1)} %wef_h.1, ...), custom_call_target="tpu_custom_call" | custom-call | tf_op jit(solution)/shard_map/pallas_call | solution.py:337
  67.3 1.0 %copy.18 = bf16[1,1024,512]{2,1,0:T(8,128)(2,1)} copy(bf16[1,1024,512]{2,1,0:T(8,128)(2,1)S(1)} %bitcast.6) | data formatting | bytes 2097152
  68.3 1.1 %copy.19 = bf16[1,1536,512]{2,1,0:T(8,128)(2,1)} copy(bf16[1,1536,512]{2,1,0:T(8,128)(2,1)S(1)} %bitcast.5) | data formatting | bytes 3145728

commit v5 on v4

--- a/solution.py
+++ b/solution.py
@@ -165,9 +165,9 @@
         if not last:
             loads["wes"].wait()
             loads["wns"].wait()
-        for c in range(4):
+        for c in range(0, 4, 2):
             forth(t, c).wait_recv()
-        for c in range(0, 4, 2):
+            forth(t, c + 1).wait_recv()
             both = flat(inc[c : c + 2])
             look[nb + c : nb + c + 2] = split(product(both, wef[D : 2 * D, :]).astype(BF16))
 
@@ -193,7 +193,7 @@
                 def _():
                     for j in range(early):
                         next_e(j).start()
-        for c in range(0, 4, 2):
+        for c in (2, 0):
             sums = product(scat[(nb + c) * B : (nb + c + 2) * B, :], msg[...]).astype(BF16)
             part[c] = sums[:B]
             part[c + 1] = sums[B:]

time: 69.6 us -> 67.4 us (0.968)
  Pallas kernels: 66.7 us -> 64.5 us
    pallas_call x1, Pallas kernels: 66.7 us -> 64.5 us  [local(): pl.pallas_call(functools.partial(kernel, n_sec, n_dom), out_shape=(pltpu....]
where the time goes in v5:
time: 67.4 us; the launch traced here: 67.2 us
  Pallas kernels  64.5 us (96%)
  local copies, waits for them, and re-layouts  2.11 us (3%)
    pallas_call x1, Pallas kernels, local(): pl.pallas_call(functools.partial(kernel, n_sec, n_dom), out_shape=(pltpu....  64.5 us
    unnamed x2, local copies, waits for them, and re-layouts  2.11 us

profile of v5, /device:TPU:2, one launch (start us, length us, event | category | flops | bytes accessed | tf_op | source)
XLA Modules:
  0.0 67.2 jit_solution(16615113017825475910)
XLA Ops:
  0.6 64.5 %shard_map.149 = (bf16[8,128,512]{2,1,0:T(8,128)(2,1)S(1)}, bf16[1536,512]{1,0:T(8,128)(2,1)S(1)}) custom-call(bf16[8,128,512]{2,1,0:T(8,128)(2,1)} %bitcast.7, bf16[1,1536,512]{2,1,0:T(8,128)(2,1)} %el.1, bf16[8,128,512]{2,1,0:T(8,128)(2,1)} %bitcast.8, bf16[1536,512]{1,0:T(8,128)(2,1)} %ee.1, bf16[1,1536,512]{2,1,0:T(8,128)(2,1)} %wef_h.1, ...), custom_call_target="tpu_custom_call" | custom-call | tf_op jit(solution)/shard_map/pallas_call | solution.py:337
  65.1 1.0 %copy.18 = bf16[1,1024,512]{2,1,0:T(8,128)(2,1)} copy(bf16[1,1024,512]{2,1,0:T(8,128)(2,1)S(1)} %bitcast.6) | data formatting | bytes 2097152
  66.1 1.1 %copy.19 = bf16[1,1536,512]{2,1,0:T(8,128)(2,1)} copy(bf16[1,1536,512]{2,1,0:T(8,128)(2,1)S(1)} %bitcast.5) | data formatting | bytes 3145728
